TPU v7x, 512 devices: a whole 4x8x8 slice. The times are simulated.
512 devices in a mesh: dom: 32 (over y, x), edge: 16 (over z, core).
Axes of the slice: x: 4, y: 8, z: 8, core: 2. Of those that a mesh axis runs over, the one named last changes fastest.
Arguments:
- left_rows: float32 [131072, 400], P(('dom', 'edge')), may hold values from -1.8 to 1.8
- left_state: float32 [131072], P(('dom', 'edge')), may hold values from 0.001 to 0.1
- right_rows: float32 [131072, 400], P(('dom', 'edge')), may hold values from -1.8 to 1.8
- right_state: float32 [131072], P(('dom', 'edge')), may hold values from 0.001 to 0.1
- relation: float32 [400], replicated, may hold values from -4 to 4
- left_rows_wanted: int32 [8192, 128], P(('dom', 'edge')), may hold values from 0 to 255
- right_rows_wanted: int32 [8192, 128], P(('dom', 'edge')), may hold values from 0 to 255
- left_edge_position: int32 [512, 1024], P(('dom', 'edge')), may hold values from 0 to 2047
- right_edge_position: int32 [512, 1024], P(('dom', 'edge')), may hold values from 0 to 2047
- negative_position: int32 [512, 512], P(('dom', 'edge')), may hold values from 0 to 2047
Outputs:
- new_left: float32 [131072, 400], P(('dom', 'edge'))
- new_left_state: float32 [131072], P(('dom', 'edge'))
- new_right: float32 [131072, 400], P(('dom', 'edge'))
- new_right_state: float32 [131072], P(('dom', 'edge'))
Inputs may be any that keep to these rules, and one draw needn't show every extreme that they name: `left_rows_wanted`: rows of the owner's 256 rows of a partition; one list may name a row more than once. `right_rows_wanted`: rows of the owner's 256 rows of a partition; one list may name a row more than once. `left_edge_position`: slot o * 128 + c is entry c of the list sent to owner o. `right_edge_position`: slot o * 128 + c is entry c of the list sent to owner o. `negative_position`: slot o * 128 + c is entry c of the list sent to owner o.
All inputs are finite; a program needn't handle non-finite values.
Results may differ from a plain program's by a relative error of at most 0.0036.
Values may be sent and summed in bfloat16 or wider, within the bound.
A program may use at most 64 MiB of HBM per device.

v0:
```python
import jax
import jax.numpy as jnp
from jax import lax
from jax.sharding import PartitionSpec as P

LEARN_RATE = 0.1
ADA_EPS = 1e-10


def passed_along(block, axis, distance):
    devices = range(lax.axis_size(axis))
    route = [((i - distance) % len(devices), i) for i in devices]
    return lax.ppermute(block, axis, route)


def complex_times(row_block, relation, sign_flip):
    half_width = row_block.shape[1] // 2
    re_rel = relation[:half_width]
    im_rel = sign_flip * relation[half_width:]
    re_row = row_block[:, :half_width]
    im_row = row_block[:, half_width:]
    return jnp.concatenate(
        [re_row * re_rel - im_row * im_rel, re_row * im_rel + im_row * re_rel], axis=1
    )


def slot_grads(
    left_slots, right_slots, left_edge_position, right_edge_position, negative_position, relation
):
    slot_count, row_width = left_slots.shape
    grad_left = jnp.zeros((slot_count, row_width), jnp.float32)
    grad_right = jnp.zeros((slot_count, row_width), jnp.float32)
    neg_count = negative_position.shape[1]
    left_idx = left_edge_position[0]
    right_idx = right_edge_position[0]
    neg_idx = negative_position[0]
    left_take = jnp.take(left_slots, left_idx, axis=0).astype(jnp.float32)
    query_rows = complex_times(left_take, relation, 1.0).astype(jnp.bfloat16)
    target = jnp.take(right_slots, right_idx, axis=0)
    sampled = jnp.take(right_slots, neg_idx, axis=0)
    positive = jnp.sum(query_rows.astype(jnp.float32) * target.astype(jnp.float32), axis=1)
    negative = lax.dot_general(
        query_rows, sampled, (((1,), (1,)), ((), ())), preferred_element_type=jnp.float32
    )
    pull_weight = -jax.nn.sigmoid(-positive)
    push_weight = (jax.nn.sigmoid(negative) / neg_count).astype(jnp.bfloat16)
    grad_query = pull_weight[:, None] * target.astype(jnp.float32) + jnp.dot(
        push_weight, sampled, preferred_element_type=jnp.float32
    )
    grad_left = grad_left.at[left_idx].add(complex_times(grad_query, relation, -1.0))
    grad_right = grad_right.at[right_idx].add(pull_weight[:, None] * query_rows.astype(jnp.float32))
    neg_grad = lax.dot_general(
        push_weight, query_rows, (((0,), (0,)), ((), ())), preferred_element_type=jnp.float32
    )
    grad_right = grad_right.at[neg_idx].add(neg_grad)
    return (grad_left.astype(jnp.bfloat16), grad_right.astype(jnp.bfloat16))


def apply_update(table, state, asked_rows, slot_grad):
    row_width = table.shape[1]
    dense = (
        jnp.zeros(table.shape, jnp.float32)
        .at[asked_rows.reshape(-1)]
        .add(slot_grad.astype(jnp.float32).reshape(-1, row_width))
    )
    state_new = state + jnp.mean(dense * dense, axis=1)
    table_new = table - LEARN_RATE * dense / (jnp.sqrt(state_new)[:, None] + ADA_EPS)
    return (table_new, state_new)


def body(
    left_rows,
    left_state,
    right_rows,
    right_state,
    relation,
    left_rows_wanted,
    right_rows_wanted,
    left_edge_position,
    right_edge_position,
    negative_position,
):
    row_width = left_rows.shape[1]
    asked_left, asked_right = (
        lax.all_to_all(left_rows_wanted, "edge", split_axis=0, concat_axis=0, tiled=True),
        lax.all_to_all(right_rows_wanted, "edge", split_axis=0, concat_axis=0, tiled=True),
    )
    sent_left = jnp.take(left_rows, asked_left, axis=0).astype(jnp.bfloat16)
    sent_right = jnp.take(right_rows, asked_right, axis=0).astype(jnp.bfloat16)
    got_left, got_right = (
        lax.all_to_all(sent_left, "edge", split_axis=0, concat_axis=0, tiled=True),
        lax.all_to_all(sent_right, "edge", split_axis=0, concat_axis=0, tiled=True),
    )
    slot_shape = got_left.shape
    slot_left, slot_right = slot_grads(
        got_left.reshape(-1, row_width),
        got_right.reshape(-1, row_width),
        left_edge_position,
        right_edge_position,
        negative_position,
        relation,
    )
    back_left, back_right = (
        lax.all_to_all(
            slot_left.reshape(slot_shape), "edge", split_axis=0, concat_axis=0, tiled=True
        ),
        lax.all_to_all(
            slot_right.reshape(slot_shape), "edge", split_axis=0, concat_axis=0, tiled=True
        ),
    )
    new_left, new_left_state = apply_update(left_rows, left_state, asked_left, back_left)
    upd_rows, upd_state = apply_update(right_rows, right_state, asked_right, back_right)
    new_right, new_right_state = passed_along((upd_rows, upd_state), "dom", 1)
    return (new_left, new_left_state, new_right, new_right_state)


def solution(mesh):
    return jax.shard_map(
        body,
        mesh=mesh,
        in_specs=(
            P(("dom", "edge"), None),
            P(("dom", "edge")),
            P(("dom", "edge"), None),
            P(("dom", "edge")),
            P(),
            P(("dom", "edge"), None),
            P(("dom", "edge"), None),
            P(("dom", "edge"), None),
            P(("dom", "edge"), None),
            P(("dom", "edge"), None),
        ),
        out_specs=(
            P(("dom", "edge"), None),
            P(("dom", "edge")),
            P(("dom", "edge"), None),
            P(("dom", "edge")),
        ),
        check_vma=False,
    )
```

profile of v0, /device:TPU:1, one launch (start us, length us, event | category | flops | bytes accessed | tf_op | source)
XLA Modules:
  0.0 284.8 jit_solution(3238225883694732752)
XLA Ops:
  0.6 11.8 %all-to-all-start = ((s32[16,1,128]{2,1,0:T(1,128)}), s32[16,1,128]{2,1,0:T(1,128)S(1)}, u32[]{:S(2)}, u32[]{:S(2)}) async-start(s32[16,1,128]{2,1,0:T(1,128)} %bitcast.56), calls=%async_computation | async-start | bytes 16384 | tf_op jit(solution)/shard_map/all_to_all | solution.py:85
  13.7 5.7 %all-to-all-done = s32[16,1,128]{2,1,0:T(1,128)S(1)} async-done(((s32[16,1,128]{2,1,0:T(1,128)}), s32[16,1,128]{2,1,0:T(1,128)S(1)}, u32[]{:S(2)}, u32[]{:S(2)}) %all-to-all-start) | async-done | bytes 8224 | tf_op jit(solution)/shard_map/all_to_all | solution.py:85
  19.4 3.9 %all-to-all-start.2 = ((s32[16,1,128]{2,1,0:T(1,128)}), s32[16,1,128]{2,1,0:T(1,128)S(1)}, u32[]{:S(2)}, u32[]{:S(2)}) async-start(s32[16,1,128]{2,1,0:T(1,128)} %bitcast.57), calls=%async_computation.2 | async-start | bytes 16384 | tf_op jit(solution)/shard_map/all_to_all | solution.py:86
  23.4 6.7 %gather_fusion.1 = bf16[2048,400]{1,0:T(8,128)(2,1)S(1)} fusion(f32[256,400]{1,0:T(8,128)S(1)} %copy.58, s32[2048]{0:T(1024)S(1)} %bitcast_clamp_fusion.1), kind=kCustom, calls=%fused_computation.clone | custom fusion | bytes 3284992 | tf_op jit(solution)/shard_map/jit(_take)/gather | solution.py:88
  32.3 2.9 %select_convert_fusion.1 = bf16[16,128,400]{1,2,0:T(8,128)(2,1)} fusion(bf16[16,128,400]{1,2,0:T(8,128)(2,1)} %copy.47, pred[16,128]{1,0:T(8,128)(4,1)S(1)} %compare_and_fusion.1), kind=kLoop, calls=%fused_computation.11 | loop fusion | flops 819200 | bytes 3278848 | tf_op jit(solution)/shard_map/convert_element_type | solution.py:88
  35.2 7.4 %all-to-all-start.1 = ((bf16[16,128,400]{1,2,0:T(8,128)(2,1)}), bf16[16,128,400]{1,2,0:T(8,128)(2,1)}, u32[]{:S(2)}, u32[]{:S(2)}) async-start(bf16[16,128,400]{1,2,0:T(8,128)(2,1)} %select_convert_fusion.1), calls=%async_computation.1 | async-start | bytes 3276800 | tf_op jit(solution)/shard_map/all_to_all | solution.py:91
  42.9 6.7 %gather_fusion.3 = bf16[2048,400]{1,0:T(8,128)(2,1)S(1)} fusion(f32[256,400]{1,0:T(8,128)S(1)} %copy.50, s32[2048]{0:T(1024)S(1)} %bitcast_clamp_fusion), kind=kCustom, calls=%fused_computation.2.clone | custom fusion | bytes 3284992 | tf_op jit(solution)/shard_map/jit(_take)/gather | solution.py:89
  51.9 3.0 %select_convert_fusion = bf16[16,128,400]{1,2,0:T(8,128)(2,1)} fusion(bf16[16,128,400]{1,2,0:T(8,128)(2,1)} %copy.51, pred[16,128]{1,0:T(8,128)(4,1)S(1)} %compare_and_fusion), kind=kLoop, calls=%fused_computation.10 | loop fusion | flops 819200 | bytes 3278848 | tf_op jit(solution)/shard_map/convert_element_type | solution.py:89
  54.8 27.7 %all-to-all-done.1 = bf16[16,128,400]{1,2,0:T(8,128)(2,1)} async-done(((bf16[16,128,400]{1,2,0:T(8,128)(2,1)}), bf16[16,128,400]{1,2,0:T(8,128)(2,1)}, u32[]{:S(2)}, u32[]{:S(2)}) %all-to-all-start.1) | async-done | bytes 1638432 | tf_op jit(solution)/shard_map/all_to_all | solution.py:91
  82.5 4.5 %all-to-all-start.3 = ((bf16[16,128,400]{1,2,0:T(8,128)(2,1)}), bf16[16,128,400]{1,2,0:T(8,128)(2,1)}, u32[]{:S(2)}, u32[]{:S(2)}) async-start(bf16[16,128,400]{1,2,0:T(8,128)(2,1)} %select_convert_fusion), calls=%async_computation.3 | async-start | bytes 3276800 | tf_op jit(solution)/shard_map/all_to_all | solution.py:92
  89.4 2.8 copy.48
  92.2 5.1 %gather_fusion.2 = bf16[1024,400]{1,0:T(8,128)(2,1)} fusion(bf16[2048,400]{1,0:T(8,128)(2,1)S(1)} %bitcast.38, s32[1024]{0:T(1024)S(1)} %fusion.10), kind=kCustom, calls=%fused_computation.1.clone | custom fusion | bytes 1642496 | tf_op jit(solution)/shard_map/jit(_take)/gather | solution.py:37
  99.5 27.2 %all-to-all-done.3 = bf16[16,128,400]{1,2,0:T(8,128)(2,1)} async-done(((bf16[16,128,400]{1,2,0:T(8,128)(2,1)}), bf16[16,128,400]{1,2,0:T(8,128)(2,1)}, u32[]{:S(2)}, u32[]{:S(2)}) %all-to-all-start.3) | async-done | bytes 1638432 | tf_op jit(solution)/shard_map/all_to_all | solution.py:92
  126.7 2.8 copy.52
  129.5 2.6 gather_fusion
  132.1 5.1 %gather_fusion.4 = bf16[1024,400]{1,0:T(8,128)(2,1)} fusion(bf16[2048,400]{1,0:T(8,128)(2,1)S(1)} %bitcast.37, s32[1024]{0:T(1024)S(1)} %fusion.11), kind=kCustom, calls=%fused_computation.3.clone | custom fusion | bytes 1642496 | tf_op jit(solution)/shard_map/jit(_take)/gather | solution.py:39
  144.3 9.5 %scatter_custom_fusion = f32[2048,400]{1,0:T(8,128)} fusion(s32[1024]{0:T(1024)} %bitcast.60, f32[1024,400]{1,0:T(8,128)} %copy.54, f32[]{:T(128)} %constant.28.clone.1), kind=kCustom, calls=%fused_computation.15 | custom fusion | flops 409600 | bytes 3277312 | tf_op jit(solution)/shard_map/scatter-add | solution.py:50
  153.7 2.5 convert_element_type.35
  158.5 4.7 %all-to-all-start.4 = ((bf16[16,128,400]{1,2,0:T(8,128)(2,1)}), bf16[16,128,400]{1,2,0:T(8,128)(2,1)}, u32[]{:S(2)}, u32[]{:S(2)}) async-start(bf16[16,128,400]{1,2,0:T(8,128)(2,1)} %copy.55), calls=%async_computation.4 | async-start | bytes 3276800 | tf_op jit(solution)/shard_map/all_to_all | solution.py:104
  165.3 9.5 %scatter_custom_fusion.2 = f32[2048,400]{1,0:T(8,128)} fusion(s32[1024]{0:T(1024)S(1)} %bitcast.61, f32[1024,400]{1,0:T(8,128)} %copy.59, f32[]{:T(128)} %constant.28.clone.1), kind=kCustom, calls=%fused_computation.13 | custom fusion | flops 409600 | bytes 3277312 | tf_op jit(solution)/shard_map/scatter-add | solution.py:51
  176.7 7.7 %scatter_fusion = f32[2048,400]{1,0:T(8,128)} fusion(f32[2048,400]{1,0:T(8,128)} %scatter_custom_fusion.2, s32[512]{0:T(512)S(1)} %bitcast.54, f32[512,400]{1,0:T(8,128)S(1)} %fusion.14), kind=kCustom, calls=%fused_computation.8 | custom fusion | flops 204800 | bytes 2459648 | tf_op jit(solution)/shard_map/scatter-add | solution.py:55
  184.5 2.5 convert_element_type.36
  189.3 13.6 %all-to-all-done.4 = bf16[16,128,400]{1,2,0:T(8,128)(2,1)} async-done(((bf16[16,128,400]{1,2,0:T(8,128)(2,1)}), bf16[16,128,400]{1,2,0:T(8,128)(2,1)}, u32[]{:S(2)}, u32[]{:S(2)}) %all-to-all-start.4) | async-done | bytes 1638432 | tf_op jit(solution)/shard_map/all_to_all | solution.py:104
  202.8 4.4 %all-to-all-start.5 = ((bf16[16,128,400]{1,2,0:T(8,128)(2,1)}), bf16[16,128,400]{1,2,0:T(8,128)(2,1)S(1)}, u32[]{:S(2)}, u32[]{:S(2)}) async-start(bf16[16,128,400]{1,2,0:T(8,128)(2,1)} %copy.61), calls=%async_computation.5 | async-start | bytes 3276800 | tf_op jit(solution)/shard_map/all_to_all | solution.py:107
  207.2 4.0 %copy.68 = f32[16,128,400]{2,1,0:T(8,128)} copy(bf16[16,128,400]{1,2,0:T(8,128)(2,1)} %all-to-all-done.4) | data formatting | bytes 4915200 | tf_op jit(solution)/shard_map/reshape | solution.py:64
  211.2 13.6 %scatter_custom_fusion.1 = f32[256,400]{1,0:T(8,128)S(1)} fusion(s32[2048]{0:T(1024)S(1)} %bitcast.59, f32[2048,400]{1,0:T(8,128)} %bitcast.44, f32[]{:T(128)} %constant.28.clone.1), kind=kCustom, calls=%fused_computation.37 | custom fusion | flops 819200 | bytes 410112 | tf_op jit(solution)/shard_map/scatter-add | solution.py:64
  225.0 21.9 %all-to-all-done.5 = bf16[16,128,400]{1,2,0:T(8,128)(2,1)S(1)} async-done(((bf16[16,128,400]{1,2,0:T(8,128)(2,1)}), bf16[16,128,400]{1,2,0:T(8,128)(2,1)S(1)}, u32[]{:S(2)}, u32[]{:S(2)}) %all-to-all-start.5) | async-done | bytes 1638432 | tf_op jit(solution)/shard_map/all_to_all | solution.py:107
  246.9 3.4 %copy.69 = f32[16,128,400]{2,1,0:T(8,128)} copy(bf16[16,128,400]{1,2,0:T(8,128)(2,1)S(1)} %all-to-all-done.5) | data formatting | bytes 4915200 | tf_op jit(solution)/shard_map/reshape | solution.py:64
  250.3 13.4 %scatter_custom_fusion.4 = f32[256,400]{1,0:T(8,128)S(1)} fusion(s32[2048]{0:T(1024)S(1)} %bitcast.58, f32[2048,400]{1,0:T(8,128)} %bitcast.43, f32[]{:T(128)} %constant.28.clone.1), kind=kCustom, calls=%fused_computation.35 | custom fusion | flops 819200 | bytes 410112 | tf_op jit(solution)/shard_map/scatter-add | solution.py:64
  264.0 3.1 %collective-permute-start = (f32[256,400]{1,0:T(8,128)S(1)}, f32[256,400]{1,0:T(8,128)S(1)}, u32[]{:S(2)}, u32[]{:S(2)}) collective-permute-start(f32[256,400]{1,0:T(8,128)S(1)} %divide_subtract_fusion), channel_id=1, source_target_pairs={{496,0},{0,16},{16,32},{32,48},{48,64},{64,80},{80,96},{96,112},{1... | collective-permute-start | bytes 1228808 | tf_op jit(solution)/shard_map/ppermute | solution.py:13
  267.1 3.1 %collective-permute-start.1 = (f32[256]{0:T(256)S(1)}, f32[256]{0:T(256)S(1)}, u32[]{:S(2)}, u32[]{:S(2)}) collective-permute-start(f32[256]{0:T(256)S(1)} %get-tuple-element.19), channel_id=1, source_target_pairs={{496,0},{0,16},{16,32},{32,48},{48,64},{64,80},{80,96},{96,112},{1... | collective-permute-start | bytes 3080 | tf_op jit(solution)/shard_map/ppermute | solution.py:13
  271.9 11.5 %collective-permute-done.1 = f32[256]{0:T(256)S(1)} collective-permute-done((f32[256]{0:T(256)S(1)}, f32[256]{0:T(256)S(1)}, u32[]{:S(2)}, u32[]{:S(2)}) %collective-permute-start.1) | collective-permute-done | bytes 1056 | tf_op jit(solution)/shard_map/ppermute | solution.py:13
  (99 shorter events, 29.8 us)
Async XLA Ops:
  0.6 18.8 %all-to-all-start = ((s32[16,1,128]{2,1,0:T(1,128)}), s32[16,1,128]{2,1,0:T(1,128)S(1)}, u32[]{:S(2)}, u32[]{:S(2)}) async-start(s32[16,1,128]{2,1,0:T(1,128)} %bitcast.56), calls=%async_computation | async-start | bytes 16384 | tf_op jit(solution)/shard_map/all_to_all | solution.py:85
  19.4 10.6 %copy-start.5 = (s32[16,1,128]{2,1,0:T(1,128)}, s32[16,1,128]{2,1,0:T(1,128)S(1)}, u32[]{:S(2)}) copy-start(s32[16,1,128]{2,1,0:T(1,128)S(1)} %all-to-all-done) | copy-start | bytes 24580
  19.4 15.8 %all-to-all-start.2 = ((s32[16,1,128]{2,1,0:T(1,128)}), s32[16,1,128]{2,1,0:T(1,128)S(1)}, u32[]{:S(2)}, u32[]{:S(2)}) async-start(s32[16,1,128]{2,1,0:T(1,128)} %bitcast.57), calls=%async_computation.2 | async-start | bytes 16384 | tf_op jit(solution)/shard_map/all_to_all | solution.py:86
  35.2 7.4 %copy-start.4 = (f32[256,400]{0,1:T(8,128)S(1)}, f32[256,400]{0,1:T(8,128)}, u32[]{:S(2)}) copy-start(f32[256,400]{0,1:T(8,128)} %param.16) | copy-start | bytes 1228804
  35.2 16.6 %copy-start.7 = (s32[16,1,128]{2,1,0:T(1,128)}, s32[16,1,128]{2,1,0:T(1,128)S(1)}, u32[]{:S(2)}) copy-start(s32[16,1,128]{2,1,0:T(1,128)S(1)} %all-to-all-done.2) | copy-start | bytes 24580
  35.2 47.3 %all-to-all-start.1 = ((bf16[16,128,400]{1,2,0:T(8,128)(2,1)}), bf16[16,128,400]{1,2,0:T(8,128)(2,1)}, u32[]{:S(2)}, u32[]{:S(2)}) async-start(bf16[16,128,400]{1,2,0:T(8,128)(2,1)} %select_convert_fusion.1), calls=%async_computation.1 | async-start | bytes 3276800 | tf_op jit(solution)/shard_map/all_to_all | solution.py:91
  54.8 32.2 %copy-start.17 = (s32[1,512]{1,0:T(1,128)S(1)}, s32[1,512]{1,0:T(1,128)}, u32[]{:S(2)}) copy-start(s32[1,512]{1,0:T(1,128)} %param.23) | copy-start | bytes 6148
  54.8 32.7 %copy-start.9 = (s32[1,1024]{1,0:T(1,128)S(1)}, s32[1,1024]{1,0:T(1,128)}, u32[]{:S(2)}) copy-start(s32[1,1024]{1,0:T(1,128)} %param.21) | copy-start | bytes 12292
  54.8 32.7 %copy-start.21 = (f32[400]{0:T(512)S(1)}, f32[400]{0:T(512)}, u32[]{:S(2)}) copy-start(f32[400]{0:T(512)} %param.18) | copy-start | bytes 4804
  54.8 33.4 %copy-start.10 = (s32[1,1024]{1,0:T(1,128)S(1)}, s32[1,1024]{1,0:T(1,128)}, u32[]{:S(2)}) copy-start(s32[1,1024]{1,0:T(1,128)} %param.22) | copy-start | bytes 12292
  82.5 44.2 %all-to-all-start.3 = ((bf16[16,128,400]{1,2,0:T(8,128)(2,1)}), bf16[16,128,400]{1,2,0:T(8,128)(2,1)}, u32[]{:S(2)}, u32[]{:S(2)}) async-start(bf16[16,128,400]{1,2,0:T(8,128)(2,1)} %select_convert_fusion), calls=%async_computation.3 | async-start | bytes 3276800 | tf_op jit(solution)/shard_map/all_to_all | solution.py:92
  87.0 2.4 copy-start.12
  137.2 1.5 copy-start.2
  137.2 1.7 copy-start.16
  137.2 1.7 copy-start.19
  138.8 1.0 copy-start.3
  138.8 1.0 copy-start.24
  139.1 1.9 copy-start
  139.9 1.2 copy-start.14
  141.0 1.0 copy-start.25
  158.5 4.7 %copy-start.11 = (s32[1,1024]{1,0:T(1,128)S(1)}, s32[1,1024]{1,0:T(1,128)}, u32[]{:S(2)}) copy-start(s32[1,1024]{1,0:T(1,128)} %param.22) | copy-start | bytes 12292
  158.5 4.7 %copy-start.1 = (bf16[1024,200]{0,1:T(8,128)(2,1)S(1)}, bf16[1024,200]{0,1:T(8,128)(2,1)}, u32[]{:S(2)}) copy-start(bf16[1024,200]{0,1:T(8,128)(2,1)} %copy-done) | copy-start | bytes 1228804
  158.5 4.7 %copy-start.15 = (f32[1024]{0:T(1024)S(1)}, f32[1024]{0:T(1024)}, u32[]{:S(2)}) copy-start(f32[1024]{0:T(1024)} %copy-done.14) | copy-start | bytes 12292
  158.5 44.3 %all-to-all-start.4 = ((bf16[16,128,400]{1,2,0:T(8,128)(2,1)}), bf16[16,128,400]{1,2,0:T(8,128)(2,1)}, u32[]{:S(2)}, u32[]{:S(2)}) async-start(bf16[16,128,400]{1,2,0:T(8,128)(2,1)} %copy.55), calls=%async_computation.4 | async-start | bytes 3276800 | tf_op jit(solution)/shard_map/all_to_all | solution.py:104
  174.8 2.0 copy-start.13
  189.2 17.9 %copy-start.6 = (s32[16,1,128]{2,1,0:T(1,128)S(1)}, s32[16,1,128]{2,1,0:T(1,128)}, u32[]{:S(2)}) copy-start(s32[16,1,128]{2,1,0:T(1,128)} %copy-done.5) | copy-start | bytes 24580
  189.3 18.0 %copy-start.8 = (s32[16,1,128]{2,1,0:T(1,128)S(1)}, s32[16,1,128]{2,1,0:T(1,128)}, u32[]{:S(2)}) copy-start(s32[16,1,128]{2,1,0:T(1,128)} %copy-done.7) | copy-start | bytes 24580
  202.8 44.1 %all-to-all-start.5 = ((bf16[16,128,400]{1,2,0:T(8,128)(2,1)}), bf16[16,128,400]{1,2,0:T(8,128)(2,1)S(1)}, u32[]{:S(2)}, u32[]{:S(2)}) async-start(bf16[16,128,400]{1,2,0:T(8,128)(2,1)} %copy.61), calls=%async_computation.5 | async-start | bytes 3276800 | tf_op jit(solution)/shard_map/all_to_all | solution.py:107
  225.0 38.8 %copy-start.22 = (f32[256]{0:T(256)S(1)}, f32[256]{0:T(256)}, u32[]{:S(2)}) copy-start(f32[256]{0:T(256)} %param.17) | copy-start | bytes 3076
  250.3 19.9 %copy-start.23 = (f32[256]{0:T(256)S(1)}, f32[256]{0:T(256)}, u32[]{:S(2)}) copy-start(f32[256]{0:T(256)} %param.15) | copy-start | bytes 3076
  264.0 19.4 %collective-permute-start = (f32[256,400]{1,0:T(8,128)S(1)}, f32[256,400]{1,0:T(8,128)S(1)}, u32[]{:S(2)}, u32[]{:S(2)}) collective-permute-start(f32[256,400]{1,0:T(8,128)S(1)} %divide_subtract_fusion), channel_id=1, source_target_pairs={{496,0},{0,16},{16,32},{32,48},{48,64},{64,80},{80,96},{96,112},{1... | collective-permute-start | bytes 1228808 | tf_op jit(solution)/shard_map/ppermute | solution.py:13
  267.1 16.2 %collective-permute-start.1 = (f32[256]{0:T(256)S(1)}, f32[256]{0:T(256)S(1)}, u32[]{:S(2)}, u32[]{:S(2)}) collective-permute-start(f32[256]{0:T(256)S(1)} %get-tuple-element.19), channel_id=1, source_target_pairs={{496,0},{0,16},{16,32},{32,48},{48,64},{64,80},{80,96},{96,112},{1... | collective-permute-start | bytes 3080 | tf_op jit(solution)/shard_map/ppermute | solution.py:13
  (2 other events, 1.6 us)
where the time goes:
time: 286 us; the launch traced here: 285 us
  waiting for transfers between devices  108 us (38%)
  other arithmetic  69.3 us (24%)
  local copies, waits for them, and re-layouts  60.1 us (21%)
  starting transfers between devices  42.9 us (15%)
  matrix products  3.84 us (1%)
    all_to_all x1, waiting for transfers between devices, body(): lax.all_to_all(sent_left, 'edge', split_axis=0, concat_axis=0, tiled=True)  27.7 us
    all_to_all x1, waiting for transfers between devices, body(): lax.all_to_all(sent_right, 'edge', split_axis=0, concat_axis=0, tiled=True)  27.2 us
    scatter-add x2, other arithmetic, apply_update(): dense = jnp.zeros(table.shape, jnp.float32).at[asked_rows.reshape(-1)].ad...  27 us
    all_to_all x1, waiting for transfers between devices, body(): lax.all_to_all(slot_right.reshape(slot_shape), 'edge', split_axis=0, conc...  21.9 us
    all_to_all x1, waiting for transfers between devices, body(): lax.all_to_all(slot_left.reshape(slot_shape), 'edge', split_axis=0, conca...  13.6 us
    all_to_all x1, starting transfers between devices, body(): lax.all_to_all(left_rows_wanted, 'edge', split_axis=0, concat_axis=0, til...  11.8 us
    ppermute x2, waiting for transfers between devices, passed_along(): return lax.ppermute(block, axis, route)  11.5 us
    scatter-add x1, other arithmetic, slot_grads(): grad_right.at[right_idx]  9.49 us
  transfers between devices with their start and end apart: 8, of which 6 were waited for; matrix products, arithmetic and copies ran while one was open for 29% of the time, Pallas kernels for 0%

commit v1 on v0

v1 whole, which is shorter than its diff:
```python
import functools

import jax
import jax.numpy as jnp
from jax import lax
from jax.experimental import pallas as pl
from jax.experimental.pallas import tpu as pltpu
from jax.sharding import PartitionSpec as P

LEARN_RATE = 0.1
ADA_EPS = 1e-10
MESH = pl.DeviceIdType.MESH
F32 = jnp.float32
BF16 = jnp.bfloat16

LEFT, RIGHT = 0, 1
HOPS = ((4, 3), (3, 4))
LANES = 128


def kernel(
    left_ref, left_state_ref, right_ref, right_state_ref, relation_ref,
    left_wanted_ref, right_wanted_ref, left_pos_ref, right_pos_ref, neg_pos_ref,
    new_left_ref, new_left_state_ref, new_right_ref, new_right_state_ref,
    tab,
    hot_left,
    hot_right,
    key_left,
    key_right,
    keyt_left,
    keyt_right,
    got_left,
    got_right,
    rel_col,
    query,
    neg_t,
    neg,
    push,
    pull,
    grad_left,
    grad_right,
    ring_out,
    ring_in,
    pair_out,
    pair_in,
    own_out,
    own_in,
    rows_in,
    state_in,
    ag_send, ag_recv, agp_send, agp_recv,
    rs_send, rs_recv, rsp_send, rsp_recv,
    misc_send, misc_recv,
):
    width, rows = left_ref.shape
    half = width // 2
    edges = left_pos_ref.shape[1]
    negs = neg_pos_ref.shape[1]
    doms = lax.axis_size("dom")
    owners = lax.axis_size("edge")
    chips = owners // 2
    dom = lax.axis_index("dom")
    me = lax.axis_index("edge")
    z = me // 2
    core = lax.rem(me, 2)
    partner = z * 2 + (1 - core)
    ring = (lax.rem(me + 2, owners), lax.rem(me + owners - 2, owners))
    next_dom = lax.rem(dom + 1, doms)
    prev_dom = lax.rem(dom + doms - 1, doms)

    barrier = pltpu.get_barrier_semaphore()
    for d, e in (
        (dom, partner), (dom, ring[0]), (dom, ring[1]),
        (prev_dom, me), (prev_dom, ring[0]), (prev_dom, ring[1]),
    ):
        pl.semaphore_signal(barrier, inc=1, device_id=(d, e), device_id_type=MESH)

    tab[LEFT, z, core] = left_ref[...].astype(BF16)
    tab[RIGHT, z, core] = right_ref[...].astype(BF16)
    pl.semaphore_wait(barrier, 6)

    started = []

    def send(src, dst, send_sem, recv_sem, d, e):
        copy = pltpu.make_async_remote_copy(
            src_ref=src, dst_ref=dst, send_sem=send_sem, recv_sem=recv_sem,
            device_id=(d, e), device_id_type=MESH,
        )
        copy.start()
        started.append(copy)
        return copy

    def at_chip(offset):
        return lax.rem(z + offset + 2 * chips, chips)

    def ring_gather(t, way, step):
        offset = -(step - 1) if way == 0 else step - 1
        block = tab.at[t, at_chip(offset), core]
        return send(block, block, ag_send.at[t, way, step - 1], ag_recv.at[t, way, step - 1], dom, ring[way])

    def pair_gather(t, slot, offset):
        block = tab.at[t, at_chip(offset), core]
        return send(block, block, agp_send.at[t, slot], agp_recv.at[t, slot], dom, partner)

    ring_copy = {}
    pair_copy = {}
    for t in (LEFT, RIGHT):
        for way in (0, 1):
            ring_copy[t, way, 1] = ring_gather(t, way, 1)
        pair_copy[t, 0] = pair_gather(t, 0, 0)
    rows_copy = send(right_ref, rows_in, misc_send.at[0], misc_recv.at[0], next_dom, me)
    state_copy = send(right_state_ref, state_in, misc_send.at[1], misc_recv.at[1], next_dom, me)

    def place(pos, wanted_ref):
        count = pos.shape[1]
        col = lax.broadcasted_iota(jnp.int32, (LANES, count), 0)
        hot = jnp.where(col == lax.rem(pos, LANES), 1.0, 0.0).astype(BF16)
        by_owner = jnp.dot(wanted_ref[...].astype(F32).astype(BF16), hot, preferred_element_type=F32)
        owner = pos // LANES
        own = lax.broadcasted_iota(jnp.int32, (owners, count), 0)
        row = jnp.sum(jnp.where(own == owner, by_owner, 0.0), axis=0, keepdims=True)
        return owner.astype(F32) * float(rows) + row

    def fill_keys(key, start, count, keyt, key_ref):
        key_ref[:, pl.ds(start, count)] = key.astype(jnp.int32)
        keyt[pl.ds(start, count), :] = jnp.transpose(jnp.broadcast_to(key, (LANES, count))).astype(jnp.int32)

    fill_keys(place(left_pos_ref[...], left_wanted_ref), 0, edges, keyt_left, key_left)
    fill_keys(place(right_pos_ref[...], right_wanted_ref), 0, edges, keyt_right, key_right)
    fill_keys(place(neg_pos_ref[...], right_wanted_ref), edges, negs, keyt_right, key_right)

    row_at = lax.broadcasted_iota(jnp.int32, (width, width), 0)
    col_at = lax.broadcasted_iota(jnp.int32, (width, width), 1)
    col = jnp.sum(jnp.where(row_at == col_at, relation_ref[...], 0.0), axis=1, keepdims=True)
    rel_col[...] = jnp.broadcast_to(col, (width, LANES))

    def fill_hot(hot, keyt, chip):
        count = keyt.shape[0]

        def step(i, _):
            at = pl.ds(pl.multiple_of(i * 256, 256), 256)
            lane = lax.broadcasted_iota(jnp.int32, (256, LANES), 1)
            for c in (0, 1):
                local = keyt[at, :] - (chip * 2 + c) * rows
                for h in range(rows // LANES):
                    hot[chip, c, at, pl.ds(h * LANES, LANES)] = jnp.where(
                        lane + h * LANES == local, 1.0, 0.0
                    ).astype(BF16)
            return 0

        lax.fori_loop(0, count // 256, step, 0)

    TILE = 512

    def take(t, chip, first):
        key_ref, got = ((key_left, got_left), (key_right, got_right))[t]
        count = key_ref.shape[1]

        def step(i, _):
            at = pl.ds(pl.multiple_of(i * TILE, TILE), TILE)
            part = None
            for c in (0, 1):
                local = key_ref[:, at] - (chip * 2 + c) * rows
                row = lax.broadcasted_iota(jnp.int32, (rows, TILE), 0)
                hot = jnp.where(row == local, 1.0, 0.0).astype(BF16)
                term = jnp.dot(tab[t, chip, c], hot, preferred_element_type=F32)
                part = term if part is None else part + term
            if first:
                got[:, at] = part
            else:
                got[:, at] += part
            return 0

        lax.fori_loop(0, count // TILE, step, 0)

    def arrive(t, step):
        for way in (0, 1):
            if step > HOPS[t][way]:
                continue
            ring_copy[t, way, step].wait_recv()
            if step < HOPS[t][way]:
                ring_copy[t, way, step + 1] = ring_gather(t, way, step + 1)
            slot = step if way == 0 else chips - step
            pair_copy[t, slot] = pair_gather(t, slot, -step if way == 0 else step)

    for chip in range(chips):
        fill_hot(hot_left, keyt_left, chip)
        fill_hot(hot_right, keyt_right, chip)
    for step in range(0, chips // 2 + 1):
        for t in (LEFT, RIGHT):
            if step > 0:
                arrive(t, step)
        for t in (LEFT, RIGHT):
            for way in (0, 1):
                if step > HOPS[t][way] or (step == 0 and way == 1):
                    continue
                offset = -step if way == 0 else step
                slot = step if way == 0 else chips - step
                pair_copy[t, slot].wait_recv()
                take(t, at_chip(offset), step == 0)

    def score(i, _):
        at = pl.ds(pl.multiple_of(i * LANES, LANES), LANES)
        pr = rel_col[:half, :]
        pi = rel_col[half:, :]
        lr = got_left[:half, at]
        li = got_left[half:, at]
        q = jnp.concatenate([lr * pr - li * pi, lr * pi + li * pr], axis=0).astype(BF16)
        query[:, at] = q
        q = q.astype(F32)
        positive = jnp.sum(q * got_right[:, at], axis=0, keepdims=True)
        weight = -jax.nn.sigmoid(-positive)
        pull[:, at] = weight
        grad_right[:, at] = (weight * q).astype(BF16)
        return 0

    lax.fori_loop(0, edges // LANES, score, 0)
    neg_cols = pl.ds(edges, negs)
    neg_t[...] = got_right[:, neg_cols].astype(BF16)
    neg[...] = jnp.transpose(got_right[:, neg_cols]).astype(BF16)

    def negatives(i, _):
        at = pl.ds(pl.multiple_of(i * 256, 256), 256)
        negative = jnp.dot(neg[...], query[:, at], preferred_element_type=F32)
        push[:, at] = (jax.nn.sigmoid(negative) * (1.0 / negs)).astype(BF16)
        return 0

    lax.fori_loop(0, edges // 256, negatives, 0)
    grad_right[:, neg_cols] = lax.dot_general(
        query[...], push[...], (((1,), (1,)), ((), ())), preferred_element_type=F32
    ).astype(BF16)

    def left_grads():
        def step(i, _):
            at = pl.ds(pl.multiple_of(i * LANES, LANES), LANES)
            pr = rel_col[:half, :]
            pi = rel_col[half:, :]
            g = pull[:, at] * got_right[:, at] + jnp.dot(neg_t[...], push[:, at], preferred_element_type=F32)
            gr = g[:half, :]
            gi = g[half:, :]
            grad_left[:, at] = jnp.concatenate([gr * pr + gi * pi, gi * pr - gr * pi], axis=0).astype(BF16)
            return 0

        lax.fori_loop(0, edges // LANES, step, 0)

    def dense(t, chip, c):
        grad, hot = ((grad_left, hot_left), (grad_right, hot_right))[t]
        return jnp.dot(grad[...], hot[chip, c], preferred_element_type=F32)

    def for_pair(t, offset):
        chip = at_chip(offset)
        slot = offset % chips
        pair_out[t, slot] = dense(t, chip, 1 - core).astype(BF16)
        pair_copy[t, slot] = send(
            pair_out.at[t, slot], pair_in.at[t, slot], rsp_send.at[t, slot], rsp_recv.at[t, slot], dom, partner
        )

    def own_part(t, offset):
        slot = offset % chips
        part = dense(t, at_chip(offset), core)
        pair_copy[t, slot].wait_recv()
        return part + pair_in[t, slot].astype(F32)

    def offset_of(t, way, step):
        far = HOPS[t][way] - step + 1
        return far if way == 0 else -far

    rs_copy = {}

    def pass_on(t, way, step):
        part = own_part(t, offset_of(t, way, step))
        if step > 1:
            rs_copy[t, way, step - 1].wait_recv()
            part = part + ring_in[t, way, step - 2].astype(F32)
        ring_out[t, way, step - 1] = part.astype(BF16)
        last = t == RIGHT and step == HOPS[t][way]
        rs_copy[t, way, step] = send(
            ring_out.at[t, way, step - 1], ring_in.at[t, way, step - 1],
            rs_send.at[t, way, step - 1], rs_recv.at[t, way, step - 1],
            next_dom if last else dom, ring[way],
        )

    for step in range(1, chips // 2 + 1):
        for t in (RIGHT, LEFT):
            if t == LEFT and step == 1:
                left_grads()
            ways = [way for way in (0, 1) if step <= HOPS[t][way]]
            for way in ways:
                for_pair(t, offset_of(t, way, step))
            for way in ways:
                pass_on(t, way, step)
    for_pair(RIGHT, 0)
    for_pair(LEFT, 0)
    own_out[...] = own_part(RIGHT, 0).astype(BF16)
    own_copy = send(own_out, own_in, misc_send.at[2], misc_recv.at[2], next_dom, me)

    def adagrad(row, state, grad, new_row_ref, new_state_ref):
        new_state = state + jnp.sum(grad * grad, axis=0, keepdims=True) * (1.0 / width)
        new_state_ref[...] = new_state
        new_row_ref[...] = row - LEARN_RATE * grad / (jnp.sqrt(new_state) + ADA_EPS)

    def from_ring(t):
        total = None
        for way in (0, 1):
            step = HOPS[t][way]
            rs_copy[t, way, step].wait_recv()
            part = ring_in[t, way, step - 1].astype(F32)
            total = part if total is None else total + part
        return total

    left_total = own_part(LEFT, 0) + from_ring(LEFT)
    adagrad(left_ref[...], left_state_ref[...], left_total, new_left_ref, new_left_state_ref)
    rows_copy.wait_recv()
    state_copy.wait_recv()
    own_copy.wait_recv()
    right_total = own_in[...].astype(F32) + from_ring(RIGHT)
    adagrad(rows_in[...], state_in[...], right_total, new_right_ref, new_right_state_ref)
    for copy in started:
        copy.wait_send()


def body(
    left_rows, left_state, right_rows, right_state, relation,
    left_rows_wanted, right_rows_wanted,
    left_edge_position, right_edge_position, negative_position,
):
    rows, width = left_rows.shape
    edges = left_edge_position.shape[1]
    negs = negative_position.shape[1]
    chips = lax.axis_size("edge") // 2
    both = edges + negs
    vmem = pl.BlockSpec(memory_space=pltpu.VMEM)
    dma = pltpu.SemaphoreType.DMA
    block = (width, rows)
    new_left, new_left_state, new_right, new_right_state = pl.pallas_call(
        kernel,
        out_shape=(
            jax.ShapeDtypeStruct(block, F32),
            jax.ShapeDtypeStruct((1, rows), F32),
            jax.ShapeDtypeStruct(block, F32),
            jax.ShapeDtypeStruct((1, rows), F32),
        ),
        in_specs=[vmem] * 10,
        out_specs=(vmem,) * 4,
        scratch_shapes=[
            pltpu.VMEM((2, chips, 2) + block, BF16),
            pltpu.VMEM((chips, 2, edges, rows), BF16),
            pltpu.VMEM((chips, 2, both, rows), BF16),
            pltpu.VMEM((1, edges), jnp.int32),
            pltpu.VMEM((1, both), jnp.int32),
            pltpu.VMEM((edges, LANES), jnp.int32),
            pltpu.VMEM((both, LANES), jnp.int32),
            pltpu.VMEM((width, edges), F32),
            pltpu.VMEM((width, both), F32),
            pltpu.VMEM((width, LANES), F32),
            pltpu.VMEM((width, edges), BF16),
            pltpu.VMEM((width, negs), BF16),
            pltpu.VMEM((negs, width), BF16),
            pltpu.VMEM((negs, edges), BF16),
            pltpu.VMEM((1, edges), F32),
            pltpu.VMEM((width, edges), BF16),
            pltpu.VMEM((width, both), BF16),
            pltpu.VMEM((2, 2, chips // 2) + block, BF16),
            pltpu.VMEM((2, 2, chips // 2) + block, BF16),
            pltpu.VMEM((2, chips) + block, BF16),
            pltpu.VMEM((2, chips) + block, BF16),
            pltpu.VMEM(block, BF16),
            pltpu.VMEM(block, BF16),
            pltpu.VMEM(block, F32),
            pltpu.VMEM((1, rows), F32),
            dma((2, 2, chips // 2)), dma((2, 2, chips // 2)), dma((2, chips)), dma((2, chips)),
            dma((2, 2, chips // 2)), dma((2, 2, chips // 2)), dma((2, chips)), dma((2, chips)),
            dma((3,)), dma((3,)),
        ],
        compiler_params=pltpu.CompilerParams(
            collective_id=0, has_side_effects=True, vmem_limit_bytes=62 * 1024 * 1024
        ),
        name="bucket_round",
    )(
        left_rows.T, left_state.reshape(1, rows), right_rows.T, right_state.reshape(1, rows),
        relation.reshape(1, width), left_rows_wanted, right_rows_wanted,
        left_edge_position, right_edge_position, negative_position,
    )
    return (new_left.T, new_left_state.reshape(rows), new_right.T, new_right_state.reshape(rows))


def solution(mesh):
    split = P(("dom", "edge"), None)
    return jax.shard_map(
        body,
        mesh=mesh,
        in_specs=(split, P(("dom", "edge")), split, P(("dom", "edge")), P(), split, split, split, split, split),
        out_specs=(split, P(("dom", "edge")), split, P(("dom", "edge"))),
        check_vma=False,
    )
```

time: 286 us -> 107 us (0.37)
  waiting for transfers between devices: 108 us -> 0 us
  Pallas kernels: 0 us -> 102 us
  other arithmetic: 69.3 us -> 0 us
  local copies, waits for them, and re-layouts: 60.1 us -> 3.72 us
  starting transfers between devices: 42.9 us -> 0 us
  matrix products: 3.84 us -> 0 us
    pallas_call x0 -> x1, Pallas kernels: none -> 102 us  [body(): pl.pallas_call(kernel, out_shape=(jax.ShapeDtypeStruct(block, F32), jax.S...]
    all_to_all x6 -> x0, waiting for transfers between devices: 96.1 us -> none  [the longest x1 27.7 us: body(): lax.all_to_all(sent_left, 'edge', split_axis=0, concat_axis=0, tiled=True)]
    scatter-add x5 -> x0, other arithmetic: 53.7 us -> none  [the longest x2 27 us: apply_update(): dense = jnp.zeros(table.shape, jnp.float32).at[asked_rows.reshape(-1)].ad...]
    all_to_all x6 -> x0, starting transfers between devices: 36.7 us -> none  [the longest x1 11.8 us: body(): lax.all_to_all(left_rows_wanted, 'edge', split_axis=0, concat_axis=0, til...]
    gather x9 -> x0, local copies, waits for them, and re-layouts: 34.4 us -> none  [the longest x2 8.97 us: body(): sent_right = jnp.take(right_rows, asked_right, axis=0).astype(jnp.bfloat16)]
    reshape x4 -> x0, local copies, waits for them, and re-layouts: 12 us -> none  [the longest x2 7.4 us: apply_update(): slot_grad.astype(jnp.float32).reshape(-1, row_width)]
    ppermute x2 -> x0, waiting for transfers between devices: 11.5 us -> none  [passed_along(): return lax.ppermute(block, axis, route)]
    convert_element_type x5 -> x0, other arithmetic: 10.9 us -> none  [the longest x2 4.91 us: slot_grads(): return (grad_left.astype(jnp.bfloat16), grad_right.astype(jnp.bfloat16))]
  transfers between devices with their start and end apart: 8 -> 0, of which waited for: 6 -> 0; matrix products, arithmetic and copies ran while one was open for 29% -> 0% of each run, Pallas kernels for 0% -> 0%
where the time goes in v1:
time: 107 us
  Pallas kernels  102 us (95%)
  local copies, waits for them, and re-layouts  3.72 us (3%)
    pallas_call x1, Pallas kernels, body(): pl.pallas_call(kernel, out_shape=(jax.ShapeDtypeStruct(block, F32), jax.S...  102 us
    unnamed x10, local copies, waits for them, and re-layouts  3.72 us

profile of v1, /device:TPU:1, one launch (start us, length us, event | category | flops | bytes accessed | tf_op | source)
XLA Modules:
  0.0 106.7 jit_solution(15908661615369876265)
XLA Ops:
  0.6 102.3 %bucket_round.1 = (f32[400,256]{1,0:T(8,128)}, f32[1,256]{1,0:T(1,128)}, f32[400,256]{1,0:T(8,128)}, f32[1,256]{1,0:T(1,128)}) custom-call(f32[400,256]{1,0:T(8,128)} %bitcast.9, f32[1,256]{1,0:T(1,128)} %bitcast.14, f32[400,256]{1,0:T(8,128)} %bitcast.10, f32[1,256]{1,0:T(1,128)} %bitcast.15, f32[1,400]{1,0:T(1,128)} %bitcast.13, ...), custom_call_target="tpu_custom_call" | custom-call | tf_op jit(solution)/shard_map/bucket_round/pallas_call | solution.py:334
  102.9 0.0 copy-start.2
  102.9 0.0 copy-start
  103.0 1.8 %copy.18 = f32[256,400]{0,1:T(8,128)} copy(f32[256,400]{0,1:T(8,128)} %bitcast.12) | data formatting | bytes 819200
  104.8 0.0 copy-done.2
  104.8 0.6 copy.19
  105.4 0.0 copy-done
  105.4 0.0 copy-start.1
  105.4 0.8 copy.20
  106.1 0.0 copy-done.1
  106.1 0.6 copy.21
Async XLA Ops:
  102.9 1.9 %copy-start.2 = (f32[1,256]{1,0:T(1,128)S(1)}, f32[1,256]{1,0:T(1,128)}, u32[]{:S(2)}) copy-start(f32[1,256]{1,0:T(1,128)} %get-tuple-element.9) | copy-start | bytes 3076
  102.9 2.4 %copy-start = (f32[400,256]{1,0:T(8,128)S(1)}, f32[400,256]{1,0:T(8,128)}, u32[]{:S(2)}) copy-start(f32[400,256]{1,0:T(8,128)} %get-tuple-element.10) | copy-start | bytes 1228804
  105.4 0.8 copy-start.1

commit v2 on v1

v2 whole, which is shorter than its diff:
```python
import jax
import jax.numpy as jnp
from jax import lax
from jax.experimental import pallas as pl
from jax.experimental.pallas import tpu as pltpu
from jax.sharding import PartitionSpec as P

LEARN_RATE = 0.1
ADA_EPS = 1e-10
MESH = pl.DeviceIdType.MESH
F32 = jnp.float32
BF16 = jnp.bfloat16

LEFT, RIGHT = 0, 1
HOPS = ((4, 3), (3, 4))
LANES = 128
STRIP = 256
CUT = 208


def round_kernel(
    left_hbm, right_hbm, right_state_hbm, relation_hbm,
    left_wanted_hbm, right_wanted_hbm, left_pos_hbm, right_pos_hbm, neg_pos_hbm,
    total_left, total_right, rows_out, state_out,
    left_ref, right_ref, relation_ref, left_wanted_ref, right_wanted_ref,
    left_pos_ref, right_pos_ref, neg_pos_ref,
    tab,
    hot_left,
    hot_right,
    key_left,
    key_right,
    keyt_left,
    keyt_right,
    got_left,
    got_right,
    rel_col,
    query,
    query_rows,
    neg_t,
    push,
    pull,
    grad_left,
    grad_right,
    mine,
    ring_out,
    ring_in,
    pair_out,
    pair_in,
    own_out,
    own_in,
    load_sem, ag_send, ag_recv, agp_send, agp_recv,
    rs_send, rs_recv, rsp_send, rsp_recv,
    misc_send, misc_recv,
):
    width, rows = left_ref.shape
    half = width // 2
    edges = left_pos_ref.shape[1]
    negs = neg_pos_ref.shape[1]
    doms = lax.axis_size("dom")
    owners = lax.axis_size("edge")
    chips = owners // 2
    far = chips // 2
    dom = lax.axis_index("dom")
    me = lax.axis_index("edge")
    z = me // 2
    core = lax.rem(me, 2)
    partner = z * 2 + (1 - core)
    ring = (lax.rem(me + 2, owners), lax.rem(me + owners - 2, owners))
    next_dom = lax.rem(dom + 1, doms)
    prev_dom = lax.rem(dom + doms - 1, doms)

    barrier = pltpu.get_barrier_semaphore()
    for d, e in (
        (dom, partner), (dom, ring[0]), (dom, ring[1]),
        (prev_dom, me), (prev_dom, ring[0]), (prev_dom, ring[1]),
    ):
        pl.semaphore_signal(barrier, inc=1, device_id=(d, e), device_id_type=MESH)

    loads = [
        pltpu.make_async_copy(src, dst, load_sem.at[i])
        for i, (src, dst) in enumerate((
            (left_hbm, left_ref), (right_hbm, right_ref), (relation_hbm, relation_ref),
            (left_wanted_hbm, left_wanted_ref), (right_wanted_hbm, right_wanted_ref),
            (left_pos_hbm, left_pos_ref), (right_pos_hbm, right_pos_ref), (neg_pos_hbm, neg_pos_ref),
        ))
    ]
    for load in loads:
        load.start()
    loads[0].wait()
    tab[LEFT, z, core] = left_ref[...].astype(BF16)
    pl.semaphore_wait(barrier, 6)

    started = []

    def send(src, dst, send_sem, recv_sem, d, e):
        copy = pltpu.make_async_remote_copy(
            src_ref=src, dst_ref=dst, send_sem=send_sem, recv_sem=recv_sem,
            device_id=(d, e), device_id_type=MESH,
        )
        copy.start()
        started.append(copy)
        return copy

    def at_chip(offset):
        return lax.rem(z + offset + 2 * chips, chips)

    PARTS = (pl.ds(0, CUT), pl.ds(CUT, width - CUT))
    ring_copy = {}
    pair_copy = {}

    def piece(t, offset, part):
        block = tab.at[t, at_chip(offset), core]
        return block if part is None else block.at[PARTS[part]]

    def ring_gather(t, way, step, part=None):
        block = piece(t, -(step - 1) if way == 0 else step - 1, part)
        sem = (t, way, step - 1, part or 0)
        ring_copy[t, way, step, part] = send(block, block, ag_send.at[sem], ag_recv.at[sem], dom, ring[way])

    def pair_gather(t, offset, part=None):
        block = piece(t, offset, part)
        sem = (t, offset % chips, part or 0)
        copy = send(block, block, agp_send.at[sem], agp_recv.at[sem], dom, partner)
        pair_copy.setdefault((t, offset % chips), []).append(copy)

    def arrive(t, step, turn=None):
        parts = [None if turn is None else (way + turn) % 2 for way in (0, 1)]
        for way in (0, 1):
            ring_copy[t, way, step, parts[way]].wait_recv()
            if step < far - 1:
                ring_gather(t, way, step + 1, parts[way])
            elif step == far - 1 and parts[way] in (None, way):
                ring_gather(t, way, far, way)
        for way in (0, 1):
            pair_gather(t, -step if way == 0 else step, parts[way])

    def from_pair(t, offset):
        for copy in pair_copy[t, offset % chips]:
            copy.wait_recv()

    for way in (0, 1):
        ring_gather(LEFT, way, 1)
    pair_gather(LEFT, 0)
    for load in loads[1:]:
        load.wait()
    tab[RIGHT, z, core] = right_ref[...].astype(BF16)

    def place(pos, wanted_ref):
        count = pos.shape[1]
        col = lax.broadcasted_iota(jnp.int32, (LANES, count), 0)
        hot = jnp.where(col == lax.rem(pos, LANES), 1.0, 0.0).astype(BF16)
        by_owner = jnp.dot(wanted_ref[...].astype(F32).astype(BF16), hot, preferred_element_type=F32)
        owner = pos // LANES
        own = lax.broadcasted_iota(jnp.int32, (owners, count), 0)
        row = jnp.sum(jnp.where(own == owner, by_owner, 0.0), axis=0, keepdims=True)
        return owner.astype(F32) * float(rows) + row

    def fill_keys(key, start, count, keyt, key_ref):
        key_ref[:, pl.ds(start, count)] = key.astype(jnp.int32)
        keyt[pl.ds(start, count), :] = jnp.transpose(jnp.broadcast_to(key, (LANES, count))).astype(jnp.int32)

    fill_keys(place(left_pos_ref[...], left_wanted_ref), 0, edges, keyt_left, key_left)
    fill_keys(place(right_pos_ref[...], right_wanted_ref), 0, edges, keyt_right, key_right)
    fill_keys(place(neg_pos_ref[...], right_wanted_ref), edges, negs, keyt_right, key_right)

    for way in (0, 1):
        ring_gather(RIGHT, way, 1, way)
    pair_gather(RIGHT, 0)
    rows_copy = send(right_ref, rows_out, misc_send.at[0], misc_recv.at[0], next_dom, me)
    state_copy = send(right_state_hbm, state_out, misc_send.at[1], misc_recv.at[1], next_dom, me)

    row_at = lax.broadcasted_iota(jnp.int32, (width, width), 0)
    col_at = lax.broadcasted_iota(jnp.int32, (width, width), 1)
    col = jnp.sum(jnp.where(row_at == col_at, relation_ref[...], 0.0), axis=1, keepdims=True)
    rel_col[...] = jnp.broadcast_to(col, (width, STRIP))

    def fill_hot(hot, keyt, chip):
        count = keyt.shape[0]

        def step(i, _):
            at = pl.ds(pl.multiple_of(i * 256, 256), 256)
            lane = lax.broadcasted_iota(jnp.int32, (256, LANES), 1)
            for c in (0, 1):
                local = keyt[at, :] - (chip * 2 + c) * rows
                for h in range(rows // LANES):
                    hot[chip, c, at, pl.ds(h * LANES, LANES)] = jnp.where(
                        lane + h * LANES == local, 1.0, 0.0
                    ).astype(BF16)
            return 0

        lax.fori_loop(0, count // 256, step, 0)

    def fill(*some):
        for chip in some:
            fill_hot(hot_left, keyt_left, chip)
            fill_hot(hot_right, keyt_right, chip)

    TILE = 512

    def take(t, offsets, first=False):
        key_ref, got = ((key_left, got_left), (key_right, got_right))[t]
        count = key_ref.shape[1]
        for offset in offsets:
            from_pair(t, offset)

        def step(i, _):
            at = pl.ds(pl.multiple_of(i * TILE, TILE), TILE)
            row = lax.broadcasted_iota(jnp.int32, (rows, TILE), 0)
            part = None
            for offset in offsets:
                chip = at_chip(offset)
                for c in (0, 1):
                    local = key_ref[:, at] - (chip * 2 + c) * rows
                    hot = jnp.where(row == local, 1.0, 0.0).astype(BF16)
                    term = jnp.dot(tab[t, chip, c], hot, preferred_element_type=F32)
                    part = term if part is None else part + term
            if first:
                got[:, at] = part
            else:
                got[:, at] += part
            return 0

        lax.fori_loop(0, count // TILE, step, 0)

    fill(0, 1, 2, 3)
    arrive(LEFT, 1)
    for way in (0, 1):
        ring_gather(RIGHT, way, 1, 1 - way)
    take(LEFT, (0,), first=True)
    take(RIGHT, (0,), first=True)
    fill(4, 5, 6, 7)
    arrive(LEFT, 2)
    arrive(RIGHT, 1, 0)
    take(LEFT, (-1, 1))
    take(LEFT, (-2, 2))
    arrive(LEFT, 3)
    arrive(RIGHT, 1, 1)
    take(RIGHT, (-1, 1))
    arrive(RIGHT, 2, 0)
    take(LEFT, (-3, 3))
    arrive(LEFT, far, 0)
    arrive(RIGHT, 2, 1)
    take(LEFT, (far,))

    def strip(i):
        return pl.ds(pl.multiple_of(i * STRIP, STRIP), STRIP)

    def make_query(i, _):
        at = strip(i)
        pr = rel_col[:half, :]
        pi = rel_col[half:, :]
        lr = got_left[:half, at]
        li = got_left[half:, at]
        q = jnp.concatenate([lr * pr - li * pi, lr * pi + li * pr], axis=0)
        query[:, at] = q.astype(BF16)
        query_rows[at, :] = jnp.transpose(q).astype(BF16)
        return 0

    lax.fori_loop(0, edges // STRIP, make_query, 0)
    arrive(RIGHT, 3, 0)
    take(RIGHT, (-2, 2))
    arrive(RIGHT, 3, 1)
    take(RIGHT, (-3, 3))
    arrive(RIGHT, far, 0)

    def last_columns(at, cores):
        chip = at_chip(far)
        row = lax.broadcasted_iota(jnp.int32, (rows, at.size), 0)
        part = got_right[:, at]
        for c in cores:
            local = key_right[:, at] - (chip * 2 + c) * rows
            hot = jnp.where(row == local, 1.0, 0.0).astype(BF16)
            part = part + jnp.dot(tab[RIGHT, chip, c], hot, preferred_element_type=F32)
        got_right[:, at] = part
        return part

    neg_cols = pl.ds(edges, negs)
    last_columns(neg_cols, (core,))
    from_pair(RIGHT, far)
    neg_t[...] = last_columns(neg_cols, (1 - core,)).astype(BF16)

    neg_total = None
    for i in range(edges // STRIP):
        at = pl.ds(i * STRIP, STRIP)
        negative = jnp.dot(query_rows[at, :], neg_t[...], preferred_element_type=F32)
        p = (jnp.tanh(negative * 0.5) * (0.5 / negs) + (0.5 / negs)).astype(BF16)
        push[at, :] = p
        term = jnp.dot(query[:, at], p, preferred_element_type=F32)
        neg_total = term if neg_total is None else neg_total + term
        q = query[:, at].astype(F32)
        positive = jnp.sum(q * last_columns(at, (0, 1)), axis=0, keepdims=True)
        weight = -jax.nn.sigmoid(-positive)
        pull[:, at] = weight
        grad_right[:, at] = (weight * q).astype(BF16)
    grad_right[:, neg_cols] = neg_total.astype(BF16)

    def left_grads():
        pr = rel_col[:half, :]
        pi = rel_col[half:, :]
        for i in range(edges // STRIP):
            at = pl.ds(i * STRIP, STRIP)
            g = pull[:, at] * got_right[:, at] + lax.dot_general(
                neg_t[...], push[at, :], (((1,), (1,)), ((), ())), preferred_element_type=F32
            )
            gr = g[:half, :]
            gi = g[half:, :]
            grad_left[:, at] = jnp.concatenate([gr * pr + gi * pi, gi * pr - gr * pi], axis=0).astype(BF16)

    def dense(t, offset, c):
        grad, hot = ((grad_left, hot_left), (grad_right, hot_right))[t]
        return jnp.dot(grad[...], hot[at_chip(offset), c], preferred_element_type=F32)

    def offset_of(t, way, step):
        left_to_go = HOPS[t][way] - step + 1
        return left_to_go if way == 0 else -left_to_go

    def ways_of(t, step):
        return [way for way in (0, 1) if step <= HOPS[t][way]]

    def give(t, offset):
        slot = offset % chips
        pair_out[t, slot] = dense(t, offset, 1 - core).astype(BF16)
        pair_copy[t, slot] = send(
            pair_out.at[t, slot], pair_in.at[t, slot], rsp_send.at[t, slot], rsp_recv.at[t, slot], dom, partner
        )

    def both_cores(t, offset):
        slot = offset % chips
        part = dense(t, offset, core)
        pair_copy[t, slot].wait_recv()
        return part + pair_in[t, slot].astype(F32)

    rs_copy = {}

    def pass_on(t, way, step, part):
        ring_out[t, way, step - 1] = part.astype(BF16)
        last = t == RIGHT and step == HOPS[t][way]
        rs_copy[t, way, step] = send(
            ring_out.at[t, way, step - 1], ring_in.at[t, way, step - 1],
            rs_send.at[t, way, step - 1], rs_recv.at[t, way, step - 1],
            next_dom if last else dom, ring[way],
        )

    def came(t, way, step):
        rs_copy[t, way, step].wait_recv()
        return ring_in[t, way, step - 1].astype(F32)

    def give_all(t, step):
        for way in ways_of(t, step):
            give(t, offset_of(t, way, step))

    def first(t):
        for way in (0, 1):
            pass_on(t, way, 1, both_cores(t, offset_of(t, way, 1)))

    def ready(t, step):
        for way in ways_of(t, step):
            mine[t, way] = both_cores(t, offset_of(t, way, step))

    def onward(t, step):
        for way in ways_of(t, step):
            pass_on(t, way, step, mine[t, way] + came(t, way, step - 1))

    give_all(RIGHT, 1)
    first(RIGHT)
    left_grads()
    give_all(LEFT, 1)
    first(LEFT)
    give_all(RIGHT, 2)
    give(RIGHT, 0)
    ready(RIGHT, 2)
    own_out[...] = both_cores(RIGHT, 0).astype(BF16)
    own_copy = send(own_out, own_in, misc_send.at[2], misc_recv.at[2], next_dom, me)
    give_all(LEFT, 2)
    for step in range(2, far + 1):
        onward(RIGHT, step)
        ready(LEFT, step)
        if step < far:
            give_all(RIGHT, step + 1)
        else:
            give(LEFT, 0)
            mine[LEFT, 1] = both_cores(LEFT, 0)
        onward(LEFT, step)
        if step < far:
            ready(RIGHT, step + 1)
            give_all(LEFT, step + 1)
    rows_copy.wait_recv()
    state_copy.wait_recv()
    own_copy.wait_recv()

    def finish(t, total):
        for way in (0, 1):
            total = total + came(t, way, HOPS[t][way])
        return total

    total_left[...] = finish(LEFT, mine[LEFT, 1])
    total_right[...] = finish(RIGHT, own_in[...].astype(F32))
    for copy in started:
        copy.wait_send()


def update_kernel(*refs):
    tables = (refs[0:3], refs[3:6])
    results = (refs[6:8], refs[8:10])
    held, made = refs[10], refs[11]
    held_state, made_state = refs[12], refs[13]
    load_sem, store_sem = refs[14], refs[15]
    width = held.shape[2]
    loads = []
    for t in (LEFT, RIGHT):
        row, state, grad = tables[t]
        loads.append([
            pltpu.make_async_copy(grad, held.at[t, 0], load_sem.at[t, 0]),
            pltpu.make_async_copy(state, held_state.at[t], load_sem.at[t, 1]),
            pltpu.make_async_copy(row, held.at[t, 1], load_sem.at[t, 2]),
        ])
        for load in loads[t]:
            load.start()
    stores = []
    for t in (LEFT, RIGHT):
        for load in loads[t]:
            load.wait()
        grad = held[t, 0]
        state = held_state[t] + jnp.sum(grad * grad, axis=0, keepdims=True) * (1.0 / width)
        made_state[t] = state
        made[t] = held[t, 1] - LEARN_RATE * grad / (jnp.sqrt(state) + ADA_EPS)
        new_row, new_state = results[t]
        for i, (src, dst) in enumerate(((made.at[t], new_row), (made_state.at[t], new_state))):
            store = pltpu.make_async_copy(src, dst, store_sem.at[t, i])
            store.start()
            stores.append(store)
    for store in stores:
        store.wait()


def body(
    left_rows, left_state, right_rows, right_state, relation,
    left_rows_wanted, right_rows_wanted,
    left_edge_position, right_edge_position, negative_position,
):
    rows, width = left_rows.shape
    edges = left_edge_position.shape[1]
    negs = negative_position.shape[1]
    owners = lax.axis_size("edge")
    chips = owners // 2
    both = edges + negs
    vmem = pl.BlockSpec(memory_space=pltpu.VMEM)
    hbm = pl.BlockSpec(memory_space=pl.ANY)
    dma = pltpu.SemaphoreType.DMA
    block = (width, rows)
    a_block = jax.ShapeDtypeStruct(block, F32)
    a_state = jax.ShapeDtypeStruct((1, rows), F32)
    left_t, right_t = left_rows.T, right_rows.T
    left_grad, right_grad, right_next, right_state_next = pl.pallas_call(
        round_kernel,
        out_shape=(a_block, a_block, a_block, a_state),
        in_specs=[hbm] * 9,
        out_specs=(vmem, vmem, hbm, hbm),
        scratch_shapes=[
            pltpu.VMEM(block, F32),
            pltpu.VMEM(block, F32),
            pltpu.VMEM((1, width), F32),
            pltpu.VMEM((owners, LANES), jnp.int32),
            pltpu.VMEM((owners, LANES), jnp.int32),
            pltpu.VMEM((1, edges), jnp.int32),
            pltpu.VMEM((1, edges), jnp.int32),
            pltpu.VMEM((1, negs), jnp.int32),
            pltpu.VMEM((2, chips, 2) + block, BF16),
            pltpu.VMEM((chips, 2, edges, rows), BF16),
            pltpu.VMEM((chips, 2, both, rows), BF16),
            pltpu.VMEM((1, edges), jnp.int32),
            pltpu.VMEM((1, both), jnp.int32),
            pltpu.VMEM((edges, LANES), jnp.int32),
            pltpu.VMEM((both, LANES), jnp.int32),
            pltpu.VMEM((width, edges), F32),
            pltpu.VMEM((width, both), F32),
            pltpu.VMEM((width, STRIP), F32),
            pltpu.VMEM((width, edges), BF16),
            pltpu.VMEM((edges, width), BF16),
            pltpu.VMEM((width, negs), BF16),
            pltpu.VMEM((edges, negs), BF16),
            pltpu.VMEM((1, edges), F32),
            pltpu.VMEM((width, edges), BF16),
            pltpu.VMEM((width, both), BF16),
            pltpu.VMEM((2, 2) + block, F32),
            pltpu.VMEM((2, 2, chips // 2) + block, BF16),
            pltpu.VMEM((2, 2, chips // 2) + block, BF16),
            pltpu.VMEM((2, chips) + block, BF16),
            pltpu.VMEM((2, chips) + block, BF16),
            pltpu.VMEM(block, BF16),
            pltpu.VMEM(block, BF16),
            dma((8,)),
            dma((2, 2, chips // 2, 2)), dma((2, 2, chips // 2, 2)), dma((2, chips, 2)), dma((2, chips, 2)),
            dma((2, 2, chips // 2)), dma((2, 2, chips // 2)), dma((2, chips)), dma((2, chips)),
            dma((3,)), dma((3,)),
        ],
        compiler_params=pltpu.CompilerParams(
            collective_id=0, has_side_effects=True, vmem_limit_bytes=62 * 1024 * 1024
        ),
        name="bucket_round",
    )(
        left_t, right_t, right_state.reshape(1, rows), relation.reshape(1, width),
        left_rows_wanted, right_rows_wanted, left_edge_position, right_edge_position, negative_position,
    )
    new_left, new_left_state, new_right, new_right_state = pl.pallas_call(
        update_kernel,
        out_shape=(a_block, a_state, a_block, a_state),
        in_specs=[hbm] * 6,
        out_specs=(hbm,) * 4,
        scratch_shapes=[
            pltpu.VMEM((2, 2) + block, F32), pltpu.VMEM((2,) + block, F32),
            pltpu.VMEM((2, 1, rows), F32), pltpu.VMEM((2, 1, rows), F32),
            dma((2, 3)), dma((2, 2)),
        ],
        name="adagrad",
    )(left_t, left_state.reshape(1, rows), left_grad, right_next, right_state_next, right_grad)
    return (new_left.T, new_left_state.reshape(rows), new_right.T, new_right_state.reshape(rows))


def solution(mesh):
    split = P(("dom", "edge"), None)
    return jax.shard_map(
        body,
        mesh=mesh,
        in_specs=(split, P(("dom", "edge")), split, P(("dom", "edge")), P(), split, split, split, split, split),
        out_specs=(split, P(("dom", "edge")), split, P(("dom", "edge"))),
        check_vma=False,
    )
```

time: 107 us -> 98.5 us (0.921)
  the two profiles are of different devices: /device:TPU:1 before, /device:TPU:31 now
where the time goes in v2:
time: 98.5 us; the launch traced here: 98.3 us
  Pallas kernels  97.5 us (99%)
    pallas_call x1, Pallas kernels, body(): pl.pallas_call(round_kernel, out_shape=(a_block, a_block, a_block, a_stat...  95.2 us
    pallas_call x1, Pallas kernels, body(): pl.pallas_call(update_kernel, out_shape=(a_block, a_state, a_block, a_sta...  2.36 us

profile of v2, /device:TPU:31, one launch (start us, length us, event | category | flops | bytes accessed | tf_op | source)
XLA Modules:
  0.0 98.3 jit_solution(6706080480529778931)
XLA Ops:
  0.6 95.2 %bucket_round.1 = (f32[400,256]{1,0:T(8,128)}, f32[400,256]{1,0:T(8,128)}, f32[400,256]{1,0:T(8,128)}, f32[1,256]{1,0:T(1,128)}) custom-call(f32[400,256]{1,0:T(8,128)} %bitcast.9, f32[400,256]{1,0:T(8,128)} %bitcast.11, f32[1,256]{1,0:T(1,128)} %bitcast.13, f32[1,400]{1,0:T(1,128)} %bitcast.12, s32[16,128]{1,0:T(8,128)} %left_wanted_hbm.1, ...), custom_call_target="tpu_custom_call" | custom-call | tf_op jit(solution)/shard_map/bucket_round/pallas_call | solution.py:454
  95.8 2.4 %adagrad.1 = (f32[400,256]{1,0:T(8,128)}, f32[1,256]{1,0:T(1,128)}, f32[400,256]{1,0:T(8,128)}, f32[1,256]{1,0:T(1,128)}) custom-call(f32[400,256]{1,0:T(8,128)} %bitcast.10, f32[1,256]{1,0:T(1,128)} %bitcast.14, f32[400,256]{1,0:T(8,128)} %get-tuple-element.12.refs_2_, f32[400,256]{1,0:T(8,128)} %get-tuple-element.13.refs_3_, ...), custom_call_target="tpu_custom_call" | custom-call | tf_op jit(solution)/shard_map/adagrad/pallas_call | solution.py:505

commit v3 on v2

--- a/solution.py
+++ b/solution.py
@@ -19,10 +19,10 @@
 
 
 def round_kernel(
-    left_hbm, right_hbm, right_state_hbm, relation_hbm,
+    left_hbm, left_state_hbm, right_hbm, right_state_hbm, relation_hbm,
     left_wanted_hbm, right_wanted_hbm, left_pos_hbm, right_pos_hbm, neg_pos_hbm,
-    total_left, total_right, rows_out, state_out,
-    left_ref, right_ref, relation_ref, left_wanted_ref, right_wanted_ref,
+    new_left_ref, new_left_state_ref, new_right_ref, new_right_state_ref,
+    left_ref, left_state_ref, right_ref, right_state_ref, relation_ref, left_wanted_ref, right_wanted_ref,
     left_pos_ref, right_pos_ref, neg_pos_ref,
     tab,
     hot_left,
@@ -48,6 +48,8 @@
     pair_in,
     own_out,
     own_in,
+    rows_in,
+    state_in,
     load_sem, ag_send, ag_recv, agp_send, agp_recv,
     rs_send, rs_recv, rsp_send, rsp_recv,
     misc_send, misc_recv,
@@ -80,6 +82,7 @@
         pltpu.make_async_copy(src, dst, load_sem.at[i])
         for i, (src, dst) in enumerate((
             (left_hbm, left_ref), (right_hbm, right_ref), (relation_hbm, relation_ref),
+            (left_state_hbm, left_state_ref), (right_state_hbm, right_state_ref),
             (left_wanted_hbm, left_wanted_ref), (right_wanted_hbm, right_wanted_ref),
             (left_pos_hbm, left_pos_ref), (right_pos_hbm, right_pos_ref), (neg_pos_hbm, neg_pos_ref),
         ))
@@ -166,8 +169,8 @@
     for way in (0, 1):
         ring_gather(RIGHT, way, 1, way)
     pair_gather(RIGHT, 0)
-    rows_copy = send(right_ref, rows_out, misc_send.at[0], misc_recv.at[0], next_dom, me)
-    state_copy = send(right_state_hbm, state_out, misc_send.at[1], misc_recv.at[1], next_dom, me)
+    rows_copy = send(right_ref, rows_in, misc_send.at[0], misc_recv.at[0], next_dom, me)
+    state_copy = send(right_state_ref, state_in, misc_send.at[1], misc_recv.at[1], next_dom, me)
 
     row_at = lax.broadcasted_iota(jnp.int32, (width, width), 0)
     col_at = lax.broadcasted_iota(jnp.int32, (width, width), 1)
@@ -276,6 +279,8 @@
 
     neg_cols = pl.ds(edges, negs)
     last_columns(neg_cols, (core,))
+    for i in range(edges // STRIP):
+        last_columns(pl.ds(i * STRIP, STRIP), (core,))
     from_pair(RIGHT, far)
     neg_t[...] = last_columns(neg_cols, (1 - core,)).astype(BF16)
 
@@ -288,16 +293,16 @@
         term = jnp.dot(query[:, at], p, preferred_element_type=F32)
         neg_total = term if neg_total is None else neg_total + term
         q = query[:, at].astype(F32)
-        positive = jnp.sum(q * last_columns(at, (0, 1)), axis=0, keepdims=True)
+        positive = jnp.sum(q * last_columns(at, (1 - core,)), axis=0, keepdims=True)
         weight = -jax.nn.sigmoid(-positive)
         pull[:, at] = weight
         grad_right[:, at] = (weight * q).astype(BF16)
     grad_right[:, neg_cols] = neg_total.astype(BF16)
 
-    def left_grads():
+    def left_grads(*strips):
         pr = rel_col[:half, :]
         pi = rel_col[half:, :]
-        for i in range(edges // STRIP):
+        for i in strips:
             at = pl.ds(i * STRIP, STRIP)
             g = pull[:, at] * got_right[:, at] + lax.dot_general(
                 neg_t[...], push[at, :], (((1,), (1,)), ((), ())), preferred_element_type=F32
@@ -310,13 +315,6 @@
         grad, hot = ((grad_left, hot_left), (grad_right, hot_right))[t]
         return jnp.dot(grad[...], hot[at_chip(offset), c], preferred_element_type=F32)
 
-    def offset_of(t, way, step):
-        left_to_go = HOPS[t][way] - step + 1
-        return left_to_go if way == 0 else -left_to_go
-
-    def ways_of(t, step):
-        return [way for way in (0, 1) if step <= HOPS[t][way]]
-
     def give(t, offset):
         slot = offset % chips
         pair_out[t, slot] = dense(t, offset, 1 - core).astype(BF16)
@@ -324,113 +322,107 @@
             pair_out.at[t, slot], pair_in.at[t, slot], rsp_send.at[t, slot], rsp_recv.at[t, slot], dom, partner
         )
 
-    def both_cores(t, offset):
+    def with_pair(t, offset, part):
         slot = offset % chips
-        part = dense(t, offset, core)
         pair_copy[t, slot].wait_recv()
         return part + pair_in[t, slot].astype(F32)
 
     rs_copy = {}
 
-    def pass_on(t, way, step, part):
-        ring_out[t, way, step - 1] = part.astype(BF16)
-        last = t == RIGHT and step == HOPS[t][way]
-        rs_copy[t, way, step] = send(
-            ring_out.at[t, way, step - 1], ring_in.at[t, way, step - 1],
-            rs_send.at[t, way, step - 1], rs_recv.at[t, way, step - 1],
-            next_dom if last else dom, ring[way],
-        )
-
-    def came(t, way, step):
-        rs_copy[t, way, step].wait_recv()
-        return ring_in[t, way, step - 1].astype(F32)
-
-    def give_all(t, step):
-        for way in ways_of(t, step):
-            give(t, offset_of(t, way, step))
+    def pass_on(t, way, step):
+        sem = (t, way, step - 1)
+        out, into = ring_out.at[sem], ring_in.at[sem]
+        if step == 1:
+            out, into = out.at[PARTS[way]], into.at[PARTS[way]]
+        last = t == RIGHT and step == far
+        rs_copy[sem] = send(out, into, rs_send.at[sem], rs_recv.at[sem], next_dom if last else dom, ring[way])
+
+    def came(t, way, step, part=slice(None)):
+        return ring_in[t, way, step - 1, part].astype(F32)
 
     def first(t):
         for way in (0, 1):
-            pass_on(t, way, 1, both_cores(t, offset_of(t, way, 1)))
+            part = PARTS[way]
+            ring_out[t, way, 0, part] = (
+                mine[t, 0, part] + pair_in[t, far, part].astype(F32)
+            ).astype(BF16)
+            pass_on(t, way, 1)
 
     def ready(t, step):
-        for way in ways_of(t, step):
-            mine[t, way] = both_cores(t, offset_of(t, way, step))
+        offsets = (far + 1 - step, step - far - 1)
+        for offset in offsets:
+            give(t, offset)
+        parts = [dense(t, offset, core) for offset in offsets]
+        for way in (0, 1):
+            mine[t, way] = with_pair(t, offsets[way], parts[way])
 
     def onward(t, step):
-        for way in ways_of(t, step):
-            pass_on(t, way, step, mine[t, way] + came(t, way, step - 1))
-
-    give_all(RIGHT, 1)
+        for way in (0, 1):
+            rs_copy[t, way, step - 2].wait_recv()
+            if step == 2:
+                part, other = PARTS[way], PARTS[1 - way]
+                ring_out[t, way, 1, part] = (mine[t, way, part] + came(t, way, 1, part)).astype(BF16)
+                ring_out[t, way, 1, other] = mine[t, way, other].astype(BF16)
+            else:
+                ring_out[t, way, step - 1] = (mine[t, way] + came(t, way, step - 1)).astype(BF16)
+            pass_on(t, way, step)
+
+    def finish(t, row, state, total):
+        for way in (0, 1):
+            rs_copy[t, way, far - 1].wait_recv()
+            total = total + came(t, way, far)
+        state = state + jnp.sum(total * total, axis=0, keepdims=True) * (1.0 / width)
+        (new_left_state_ref, new_right_state_ref)[t][...] = state
+        (new_left_ref, new_right_ref)[t][...] = row - LEARN_RATE * total / (jnp.sqrt(state) + ADA_EPS)
+
+    strips = range(edges // STRIP)
+    give(RIGHT, far)
+    mine[RIGHT, 0] = dense(RIGHT, far, core)
+    left_grads(*strips[:-1])
+    pair_copy[RIGHT, far].wait_recv()
     first(RIGHT)
-    left_grads()
-    give_all(LEFT, 1)
+    left_grads(*strips[-1:])
+    give(LEFT, far)
+    mine[LEFT, 0] = dense(LEFT, far, core)
+    ready_right = (far - 1, 1 - far)
+    for offset in ready_right:
+        give(RIGHT, offset)
+    pair_copy[LEFT, far].wait_recv()
     first(LEFT)
-    give_all(RIGHT, 2)
+    for way in (0, 1):
+        mine[RIGHT, way] = with_pair(RIGHT, ready_right[way], dense(RIGHT, ready_right[way], core))
+    onward(RIGHT, 2)
+    ready(LEFT, 2)
     give(RIGHT, 0)
-    ready(RIGHT, 2)
-    own_out[...] = both_cores(RIGHT, 0).astype(BF16)
+    onward(LEFT, 2)
+    own_out[...] = with_pair(RIGHT, 0, dense(RIGHT, 0, core)).astype(BF16)
     own_copy = send(own_out, own_in, misc_send.at[2], misc_recv.at[2], next_dom, me)
-    give_all(LEFT, 2)
-    for step in range(2, far + 1):
-        onward(RIGHT, step)
-        ready(LEFT, step)
-        if step < far:
-            give_all(RIGHT, step + 1)
-        else:
-            give(LEFT, 0)
-            mine[LEFT, 1] = both_cores(LEFT, 0)
-        onward(LEFT, step)
-        if step < far:
-            ready(RIGHT, step + 1)
-            give_all(LEFT, step + 1)
+    ready(RIGHT, 3)
+    onward(RIGHT, 3)
+    ready(LEFT, 3)
+    onward(LEFT, 3)
+    ready(RIGHT, 4)
+    onward(RIGHT, 4)
+    ready(LEFT, 4)
+    onward(LEFT, 4)
+    give(LEFT, 0)
+    mine[LEFT, 2] = with_pair(LEFT, 0, dense(LEFT, 0, core))
     rows_copy.wait_recv()
     state_copy.wait_recv()
     own_copy.wait_recv()
-
-    def finish(t, total):
-        for way in (0, 1):
-            total = total + came(t, way, HOPS[t][way])
-        return total
-
-    total_left[...] = finish(LEFT, mine[LEFT, 1])
-    total_right[...] = finish(RIGHT, own_in[...].astype(F32))
+    finish(RIGHT, rows_in[...], state_in[...], own_in[...].astype(F32))
+    finish(LEFT, left_ref[...], left_state_ref[...], mine[LEFT, 2])
     for copy in started:
         copy.wait_send()
 
 
-def update_kernel(*refs):
-    tables = (refs[0:3], refs[3:6])
-    results = (refs[6:8], refs[8:10])
-    held, made = refs[10], refs[11]
-    held_state, made_state = refs[12], refs[13]
-    load_sem, store_sem = refs[14], refs[15]
-    width = held.shape[2]
-    loads = []
-    for t in (LEFT, RIGHT):
-        row, state, grad = tables[t]
-        loads.append([
-            pltpu.make_async_copy(grad, held.at[t, 0], load_sem.at[t, 0]),
-            pltpu.make_async_copy(state, held_state.at[t], load_sem.at[t, 1]),
-            pltpu.make_async_copy(row, held.at[t, 1], load_sem.at[t, 2]),
-        ])
-        for load in loads[t]:
-            load.start()
-    stores = []
-    for t in (LEFT, RIGHT):
-        for load in loads[t]:
-            load.wait()
-        grad = held[t, 0]
-        state = held_state[t] + jnp.sum(grad * grad, axis=0, keepdims=True) * (1.0 / width)
-        made_state[t] = state
-        made[t] = held[t, 1] - LEARN_RATE * grad / (jnp.sqrt(state) + ADA_EPS)
-        new_row, new_state = results[t]
-        for i, (src, dst) in enumerate(((made.at[t], new_row), (made_state.at[t], new_state))):
-            store = pltpu.make_async_copy(src, dst, store_sem.at[t, i])
-            store.start()
-            stores.append(store)
-    for store in stores:
-        store.wait()
+def place_kernel(*refs):
+    sems = refs[-1]
+    copies = [pltpu.make_async_copy(refs[i], refs[4 + i], sems.at[i]) for i in range(4)]
+    for copy in copies:
+        copy.start()
+    for copy in copies:
+        copy.wait()
 
 
 def body(
@@ -444,21 +436,22 @@
     owners = lax.axis_size("edge")
     chips = owners // 2
     both = edges + negs
+    hbm = pl.BlockSpec(memory_space=pl.ANY)
     vmem = pl.BlockSpec(memory_space=pltpu.VMEM)
-    hbm = pl.BlockSpec(memory_space=pl.ANY)
     dma = pltpu.SemaphoreType.DMA
     block = (width, rows)
     a_block = jax.ShapeDtypeStruct(block, F32)
     a_state = jax.ShapeDtypeStruct((1, rows), F32)
-    left_t, right_t = left_rows.T, right_rows.T
-    left_grad, right_grad, right_next, right_state_next = pl.pallas_call(
+    made = pl.pallas_call(
         round_kernel,
-        out_shape=(a_block, a_block, a_block, a_state),
-        in_specs=[hbm] * 9,
-        out_specs=(vmem, vmem, hbm, hbm),
+        out_shape=(pltpu.VMEM(block, F32), pltpu.VMEM((1, rows), F32), pltpu.VMEM(block, F32), pltpu.VMEM((1, rows), F32)),
+        in_specs=[hbm] * 10,
+        out_specs=(vmem,) * 4,
         scratch_shapes=[
             pltpu.VMEM(block, F32),
+            pltpu.VMEM((1, rows), F32),
             pltpu.VMEM(block, F32),
+            pltpu.VMEM((1, rows), F32),
             pltpu.VMEM((1, width), F32),
             pltpu.VMEM((owners, LANES), jnp.int32),
             pltpu.VMEM((owners, LANES), jnp.int32),
@@ -482,38 +475,37 @@
             pltpu.VMEM((1, edges), F32),
             pltpu.VMEM((width, edges), BF16),
             pltpu.VMEM((width, both), BF16),
-            pltpu.VMEM((2, 2) + block, F32),
+            pltpu.VMEM((2, 3) + block, F32),
             pltpu.VMEM((2, 2, chips // 2) + block, BF16),
             pltpu.VMEM((2, 2, chips // 2) + block, BF16),
             pltpu.VMEM((2, chips) + block, BF16),
             pltpu.VMEM((2, chips) + block, BF16),
             pltpu.VMEM(block, BF16),
             pltpu.VMEM(block, BF16),
-            dma((8,)),
+            pltpu.VMEM(block, F32),
+            pltpu.VMEM((1, rows), F32),
+            dma((10,)),
             dma((2, 2, chips // 2, 2)), dma((2, 2, chips // 2, 2)), dma((2, chips, 2)), dma((2, chips, 2)),
             dma((2, 2, chips // 2)), dma((2, 2, chips // 2)), dma((2, chips)), dma((2, chips)),
             dma((3,)), dma((3,)),
         ],
         compiler_params=pltpu.CompilerParams(
-            collective_id=0, has_side_effects=True, vmem_limit_bytes=62 * 1024 * 1024
+            collective_id=0, has_side_effects=True, vmem_limit_bytes=58 * 1024 * 1024
         ),
         name="bucket_round",
     )(
-        left_t, right_t, right_state.reshape(1, rows), relation.reshape(1, width),
-        left_rows_wanted, right_rows_wanted, left_edge_position, right_edge_position, negative_position,
+        left_rows.T, left_state.reshape(1, rows), right_rows.T, right_state.reshape(1, rows),
+        relation.reshape(1, width), left_rows_wanted, right_rows_wanted,
+        left_edge_position, right_edge_position, negative_position,
     )
     new_left, new_left_state, new_right, new_right_state = pl.pallas_call(
-        update_kernel,
+        place_kernel,
         out_shape=(a_block, a_state, a_block, a_state),
-        in_specs=[hbm] * 6,
+        in_specs=[vmem] * 4,
         out_specs=(hbm,) * 4,
-        scratch_shapes=[
-            pltpu.VMEM((2, 2) + block, F32), pltpu.VMEM((2,) + block, F32),
-            pltpu.VMEM((2, 1, rows), F32), pltpu.VMEM((2, 1, rows), F32),
-            dma((2, 3)), dma((2, 2)),
-        ],
-        name="adagrad",
-    )(left_t, left_state.reshape(1, rows), left_grad, right_next, right_state_next, right_grad)
+        scratch_shapes=[dma((4,))],
+        name="place",
+    )(*(pltpu.with_memory_space_constraint(x, pltpu.VMEM) for x in made))
     return (new_left.T, new_left_state.reshape(rows), new_right.T, new_right_state.reshape(rows))
 
 

time: 98.5 us -> 90.2 us (0.916)
  the two profiles are of different devices: /device:TPU:31 before, /device:TPU:1 now
where the time goes in v3:
time: 90.2 us; the launch traced here: 90.1 us
  Pallas kernels  89.3 us (99%)
    pallas_call x1, Pallas kernels, body(): pl.pallas_call(round_kernel, out_shape=(pltpu.VMEM(block, F32), pltpu.VME...  88.4 us

profile of v3, /device:TPU:1, one launch (start us, length us, event | category | flops | bytes accessed | tf_op | source)
XLA Modules:
  0.0 90.1 jit_solution(12293541420992651886)
XLA Ops:
  0.6 88.4 %bucket_round.1 = (f32[400,256]{1,0:T(8,128)S(1)}, f32[1,256]{1,0:T(1,128)S(1)}, f32[400,256]{1,0:T(8,128)S(1)}, f32[1,256]{1,0:T(1,128)S(1)}) custom-call(f32[400,256]{1,0:T(8,128)} %bitcast.9, f32[1,256]{1,0:T(1,128)} %bitcast.12, f32[400,256]{1,0:T(8,128)} %bitcast.10, f32[1,256]{1,0:T(1,128)} %bitcast.13, f32[1,400]{1,0:T(1,128)} %bitcast.11, ...), custom_call_target="tpu_custom_call" | custom-call | tf_op jit(solution)/shard_map/bucket_round/pallas_call | solution.py:445
  89.0 0.9 %place.1 = (f32[400,256]{1,0:T(8,128)}, f32[1,256]{1,0:T(1,128)}, f32[400,256]{1,0:T(8,128)}, f32[1,256]{1,0:T(1,128)}) custom-call(f32[400,256]{1,0:T(8,128)S(1)} %get-tuple-element.12.refs_0_, f32[1,256]{1,0:T(1,128)S(1)} %get-tuple-element.13.refs_1_, f32[400,256]{1,0:T(8,128)S(1)} %get-tuple-element.14.refs_2_, f32[1,256]{1,0:T(1,128)S(1)} %get-tuple-element.15.refs_3_), custom_call_target="tpu_custom_call" | custom-call | tf_op jit(solution)/shard_map/place/pallas_call | solution.py:501

commit v4 on v3

--- a/solution.py
+++ b/solution.py
@@ -223,7 +223,7 @@
                 got[:, at] += part
             return 0
 
-        lax.fori_loop(0, count // TILE, step, 0)
+        lax.fori_loop(0, count // TILE, step, 0, unroll=True)
 
     fill(0, 1, 2, 3)
     arrive(LEFT, 1)
@@ -259,7 +259,7 @@
         query_rows[at, :] = jnp.transpose(q).astype(BF16)
         return 0
 
-    lax.fori_loop(0, edges // STRIP, make_query, 0)
+    lax.fori_loop(0, edges // STRIP, make_query, 0, unroll=True)
     arrive(RIGHT, 3, 0)
     take(RIGHT, (-2, 2))
     arrive(RIGHT, 3, 1)
@@ -284,20 +284,17 @@
     from_pair(RIGHT, far)
     neg_t[...] = last_columns(neg_cols, (1 - core,)).astype(BF16)
 
-    neg_total = None
-    for i in range(edges // STRIP):
+    strips = range(edges // STRIP)
+    for i in strips:
         at = pl.ds(i * STRIP, STRIP)
         negative = jnp.dot(query_rows[at, :], neg_t[...], preferred_element_type=F32)
-        p = (jnp.tanh(negative * 0.5) * (0.5 / negs) + (0.5 / negs)).astype(BF16)
-        push[at, :] = p
-        term = jnp.dot(query[:, at], p, preferred_element_type=F32)
-        neg_total = term if neg_total is None else neg_total + term
+        push[at, :] = (jnp.tanh(negative * 0.5) * (0.5 / negs) + (0.5 / negs)).astype(BF16)
         q = query[:, at].astype(F32)
         positive = jnp.sum(q * last_columns(at, (1 - core,)), axis=0, keepdims=True)
         weight = -jax.nn.sigmoid(-positive)
         pull[:, at] = weight
         grad_right[:, at] = (weight * q).astype(BF16)
-    grad_right[:, neg_cols] = neg_total.astype(BF16)
+    grad_right[:, neg_cols] = jnp.dot(query[...], push[...], preferred_element_type=F32).astype(BF16)
 
     def left_grads(*strips):
         pr = rel_col[:half, :]
@@ -375,7 +372,6 @@
         (new_left_state_ref, new_right_state_ref)[t][...] = state
         (new_left_ref, new_right_ref)[t][...] = row - LEARN_RATE * total / (jnp.sqrt(state) + ADA_EPS)
 
-    strips = range(edges // STRIP)
     give(RIGHT, far)
     mine[RIGHT, 0] = dense(RIGHT, far, core)
     left_grads(*strips[:-1])

time: 90.2 us -> 90.6 us (level); the launches traced: 90.1 us -> 89.6 us
  no operation moved by 1% of the time
where the time goes in v4:
time: 90.6 us; the launch traced here: 89.6 us
  Pallas kernels  88.8 us (98%)
    pallas_call x1, Pallas kernels, body(): pl.pallas_call(round_kernel, out_shape=(pltpu.VMEM(block, F32), pltpu.VME...  87.8 us

profile of v4, /device:TPU:1, one launch (start us, length us, event | category | flops | bytes accessed | tf_op | source)
XLA Modules:
  0.0 89.6 jit_solution(8475220269715830736)
XLA Ops:
  0.6 87.8 %bucket_round.1 = (f32[400,256]{1,0:T(8,128)S(1)}, f32[1,256]{1,0:T(1,128)S(1)}, f32[400,256]{1,0:T(8,128)S(1)}, f32[1,256]{1,0:T(1,128)S(1)}) custom-call(f32[400,256]{1,0:T(8,128)} %bitcast.9, f32[1,256]{1,0:T(1,128)} %bitcast.12, f32[400,256]{1,0:T(8,128)} %bitcast.10, f32[1,256]{1,0:T(1,128)} %bitcast.13, f32[1,400]{1,0:T(1,128)} %bitcast.11, ...), custom_call_target="tpu_custom_call" | custom-call | tf_op jit(solution)/shard_map/bucket_round/pallas_call | solution.py:441
  88.5 0.9 %place.1 = (f32[400,256]{1,0:T(8,128)}, f32[1,256]{1,0:T(1,128)}, f32[400,256]{1,0:T(8,128)}, f32[1,256]{1,0:T(1,128)}) custom-call(f32[400,256]{1,0:T(8,128)S(1)} %get-tuple-element.12.refs_0_, f32[1,256]{1,0:T(1,128)S(1)} %get-tuple-element.13.refs_1_, f32[400,256]{1,0:T(8,128)S(1)} %get-tuple-element.14.refs_2_, f32[1,256]{1,0:T(1,128)S(1)} %get-tuple-element.15.refs_3_), custom_call_target="tpu_custom_call" | custom-call | tf_op jit(solution)/shard_map/place/pallas_call | solution.py:497
